TPU v7x, 32 devices: a whole 2x2x4 slice. The times are simulated.
32 devices in a mesh: ctx: 8 (over z, y), tp: 4 (over x, core).
Axes of the slice: x: 2, y: 2, z: 4, core: 2. Of those that a mesh axis runs over, the one named last changes fastest.
Arguments:
- queries: bfloat16 [512, 3584], P('ctx', 'tp'), may hold values from -6 to 6
- keys: bfloat16 [512, 512], P('ctx', 'tp'), may hold values from -5 to 5
- values: bfloat16 [512, 512], P('ctx', 'tp'), may hold values from -6 to 6
- block_table: int32 [8], replicated, may hold values from 0 to 7, each once
- residual: bfloat16 [512, 3584], P(('ctx', 'tp')), may hold values from -6 to 6
- out_weight: bfloat16 [3584, 3584], P('tp'), may hold values from -0.5 to 0.5
- norm_gain: bfloat16 [3584], replicated, may hold values from 0.099609375 to 1.8984375
- gate_logit_weight: bfloat16 [3584], replicated, may hold values from -0.09375 to 0.09375
- gate_weight: bfloat16 [3584, 20480], P(None, 'ctx'), may hold values from -0.09375 to 0.09375
- up_weight: bfloat16 [3584, 20480], P(None, 'ctx'), may hold values from -0.09375 to 0.09375
- down_weight: bfloat16 [20480, 3584], P('ctx'), may hold values from -0.0390625 to 0.0390625
Outputs:
- layer_out: bfloat16 [512, 3584], P(('ctx', 'tp'))
Inputs may be any that keep to these rules, and one draw needn't show every extreme that they name: Each entry names a different pair; slot c holds blocks block_table[c] and its mirror, counted from the end of the prompt.
All inputs are finite; a program needn't handle non-finite values.
Results may differ from a plain program's by a relative error of at most 0.017.
Values may be sent and summed in bfloat16 or wider, within the bound.
A program may use at most 128 MiB of HBM per device.

v0:
```python
import jax
import jax.numpy as jnp
from jax import lax
from jax.sharding import PartitionSpec as P

HEADS = 28
KV_HEADS = 4
HEAD_DIM = 128


def per_device(
    queries,
    keys,
    values,
    block_table,
    residual,
    out_weight,
    norm_gain,
    gate_logit_weight,
    gate_weight,
    up_weight,
    down_weight,
):
    tokens = queries.shape[0]
    half = tokens // 2
    ctx_count = lax.axis_size("ctx")
    tp_count = lax.axis_size("tp")
    quarter = tokens // tp_count
    group = HEADS // KV_HEADS
    kv_local = keys.shape[1] // HEAD_DIM
    scale = HEAD_DIM ** (-0.5)
    mirror = 2 * ctx_count - 1
    slots = jnp.arange(ctx_count, dtype=jnp.int32)

    def row_positions(first_row, count):
        rows = first_row + jnp.arange(count, dtype=jnp.int32)
        owner = rows // tokens
        local = rows % tokens
        onehot = (owner[:, None] == slots[None, :]).astype(jnp.int32)
        pair = jnp.sum(onehot * block_table[None, :], axis=1)
        return jnp.where(local < half, pair * half + local, (mirror - pair) * half + local - half)

    own_place = row_positions(lax.axis_index("ctx") * tokens, tokens)
    query_heads = queries.reshape(tokens, kv_local, group, HEAD_DIM)
    start_max = jnp.full((kv_local, group, tokens), -1e30, jnp.float32)
    key_piece = lax.all_gather(keys, "ctx", axis=0, tiled=True)
    value_piece = lax.all_gather(values, "ctx", axis=0, tiled=True)
    count = key_piece.shape[0]
    key_place = row_positions(jnp.int32(0), count)
    key_heads = key_piece.reshape(count, kv_local, HEAD_DIM)
    value_heads = value_piece.reshape(count, kv_local, HEAD_DIM)
    score = (
        jnp.einsum("tkgd,pkd->kgtp", query_heads, key_heads, preferred_element_type=jnp.float32)
        * scale
    )
    visible = key_place[None, :] <= own_place[:, None]
    score = jnp.where(visible, score, -1e30)
    new_max = jnp.maximum(start_max, jnp.max(score, axis=-1))
    weight = jnp.where(visible, jnp.exp(score - new_max[..., None]), 0.0)
    new_sum = jnp.sum(weight, axis=-1)
    added = jnp.einsum(
        "kgtp,pkd->kgtd",
        weight.astype(jnp.bfloat16),
        value_heads,
        preferred_element_type=jnp.float32,
    )
    summed = added / new_sum[..., None]
    attended_heads = (
        jnp.transpose(summed, (2, 0, 1, 3))
        .astype(jnp.bfloat16)
        .reshape(tokens, kv_local * group * HEAD_DIM)
    )
    projected = jnp.dot(attended_heads, out_weight, preferred_element_type=jnp.float32)
    total = lax.psum(projected.astype(jnp.bfloat16), "tp").astype(jnp.float32)
    head_sum = lax.dynamic_slice_in_dim(total, lax.axis_index("tp") * quarter, quarter, 0)
    attended = (residual.astype(jnp.float32) + head_sum).astype(jnp.bfloat16)
    attended = lax.optimization_barrier(attended)
    attended_f = attended.astype(jnp.float32)
    mean_square = jnp.mean(attended_f * attended_f, axis=-1, keepdims=True)
    normed = (attended_f * lax.rsqrt(mean_square + 1e-06) * norm_gain.astype(jnp.float32)).astype(
        jnp.bfloat16
    )
    gate_prob = jax.nn.sigmoid(
        jnp.dot(normed, gate_logit_weight, preferred_element_type=jnp.float32)
    )
    piece = lax.all_gather(normed, "ctx", axis=0, tiled=True)
    gate_part = jnp.dot(piece, gate_weight, preferred_element_type=jnp.float32)
    up_part = jnp.dot(piece, up_weight, preferred_element_type=jnp.float32)
    hidden = (jax.nn.silu(gate_part) * up_part).astype(jnp.bfloat16)
    rows = hidden
    shared = lax.psum_scatter(
        jnp.dot(rows, down_weight, preferred_element_type=jnp.float32),
        "ctx",
        scatter_dimension=0,
        tiled=True,
    )
    return (attended_f + gate_prob[:, None] * shared).astype(jnp.bfloat16)


def solution(mesh):
    return jax.shard_map(
        per_device,
        mesh=mesh,
        in_specs=(
            P("ctx", "tp"),
            P("ctx", "tp"),
            P("ctx", "tp"),
            P(),
            P(("ctx", "tp"), None),
            P("tp", None),
            P(),
            P(),
            P(None, "ctx"),
            P(None, "ctx"),
            P("ctx", None),
        ),
        out_specs=P(("ctx", "tp"), None),
        check_vma=False,
    )
```

profile of v0, /device:TPU:0, one launch (start us, length us, event | category | flops | bytes accessed | tf_op | source)
XLA Modules:
  0.0 247.7 jit_solution(735881765121248301)
XLA Ops:
  6.6 0.8 select_reduce_fusion.1
  7.4 0.7 select_reduce_fusion
  8.2 32.6 %all_gather.9 = bf16[512,128]{1,0:T(8,128)(2,1)S(1)} all-gather(bf16[64,128]{1,0:T(8,128)(2,1)} %param.12), channel_id=1, replica_groups=mesh['ctx'=8,'tp'=4] {'ctx'}, dimensions={0}, use_global_device_ids=true | all-gather | bytes 147456 | tf_op jit(solution)/shard_map/all_gather | solution.py:46
  40.8 30.7 %all_gather.10 = bf16[512,128]{1,0:T(8,128)(2,1)S(1)} all-gather(bf16[64,128]{1,0:T(8,128)(2,1)} %param.13), channel_id=1, replica_groups=mesh['ctx'=8,'tp'=4] {'ctx'}, dimensions={0}, use_global_device_ids=true | all-gather | bytes 147456 | tf_op jit(solution)/shard_map/all_gather | solution.py:47
  71.5 0.1 broadcast_compare_fusion
  71.6 0.4 fusion.35
  71.9 0.3 fusion.9
  72.3 0.3 fusion.4
  72.6 0.1 copy.16
  72.7 4.9 %convolution_convert_fusion = bf16[64,3584]{1,0:T(8,128)(2,1)} fusion(bf16[896,3584]{1,0:T(8,128)(2,1)} %param.16, bf16[8,8,7,128]{3,2,1,0:T(8,128)(2,1)S(1)} %bitcast.54), kind=kOutput, calls=%fused_computation | convolution fusion | flops 411271168 | bytes 6995968 | tf_op jit(solution)/shard_map/dot_general | solution.py:73
  77.6 0.0 all-reduce.2.cloned.1.call-update
  77.6 0.0 reduce-scatter.2.cloned.1.call-start
  77.7 33.9 %all-reduce.2.cloned.1.call-done = bf16[64,3584]{1,0:T(8,128)(2,1)} async-done(((bf16[64,3584]{1,0:T(8,128)(2,1)}), bf16[64,3584]{1,0:T(8,128)(2,1)}) %all-reduce.2.cloned.1.call-update) | async-done | bytes 458768 | tf_op jit(solution)/shard_map/psum | solution.py:74
  111.5 0.9 add_convert_fusion
  112.5 0.1 fusion.17
  112.6 0.1 fusion.19
  112.7 32.6 %all_gather.11 = bf16[128,3584]{1,0:T(8,128)(2,1)S(1)} all-gather(bf16[16,3584]{1,0:T(8,128)(2,1)S(1)} %fusion.19), channel_id=1, replica_groups=mesh['ctx'=8,'tp'=4] {'ctx'}, dimensions={0}, use_global_device_ids=true | all-gather | bytes 1032192 | tf_op jit(solution)/shard_map/all_gather | solution.py:86
  145.4 8.8 %fusion.36 = f32[128,2560]{1,0:T(8,128)S(1)} fusion(bf16[128,3584]{1,0:T(8,128)(2,1)S(1)} %all_gather.11, bf16[3584,2560]{1,0:T(8,128)(2,1)} %param.19), kind=kOutput, calls=%fused_computation.65 | convolution fusion | flops 2348810240 | bytes 20578304 | tf_op jit(solution)/shard_map/dot_general | solution.py:87
  154.1 0.0 copy-start.4
  154.2 18.0 %fusion.11 = f32[128,3584]{1,0:T(8,128)} fusion(bf16[2560,3584]{1,0:T(8,128)(2,1)} %param.21, bf16[128,3584]{1,0:T(8,128)(2,1)S(1)} %all_gather.11, bf16[3584,2560]{1,0:T(8,128)(2,1)} %param.20, f32[128,2560]{1,0:T(8,128)S(1)} %fusion.36), kind=kOutput, calls=%fused_computation.17 | convolution fusion | flops 4699586560 | bytes 40763392 | tf_op jit(solution)/shard_map/dot_general | solution.py:92
  172.1 0.0 reduce-scatter.2.cloned.1.call-update
  172.2 0.1 fusion.8
  172.3 66.8 %reduce-scatter.2.cloned.1.call-done = f32[16,3584]{1,0:T(8,128)} async-done(((f32[128,3584]{1,0:T(8,128)}), f32[16,3584]{1,0:T(8,128)}) %reduce-scatter.2.cloned.1.call-update) | async-done | bytes 229392 | tf_op jit(solution)/shard_map/reduce_scatter | solution.py:91
  239.2 1.7 fusion.20
  (18 shorter events, 0.1 us)
Async XLA Ops:
  6.5 65.0 %copy-start = (bf16[64,896]{1,0:T(8,128)(2,1)S(1)}, bf16[64,896]{1,0:T(8,128)(2,1)}, u32[]{:S(2)}) copy-start(bf16[64,896]{1,0:T(8,128)(2,1)} %param.11) | copy-start | bytes 344068
  6.5 71.1 %copy-start.3 = (bf16[3584]{0:T(1024)(128)(2,1)S(1)}, bf16[3584]{0:T(1024)(128)(2,1)}, u32[]{:S(2)}) copy-start(bf16[3584]{0:T(1024)(128)(2,1)} %param.17) | copy-start | bytes 21508
  6.5 105.0 %copy-start.2 = (bf16[16,3584]{1,0:T(8,128)(2,1)S(1)}, bf16[16,3584]{1,0:T(8,128)(2,1)}, u32[]{:S(2)}) copy-start(bf16[16,3584]{1,0:T(8,128)(2,1)} %param.15) | copy-start | bytes 344068
  6.5 105.0 %all-reduce.2.cloned.1.call-start = ((), (), s32[]{:S(2)}) async-start(), calls=%async_computation.1 | async-start | bytes 917504 | tf_op jit(solution)/shard_map/psum | solution.py:74
  77.6 161.6 %reduce-scatter.2.cloned.1.call-start = ((), (), s32[]{:S(2)}) async-start(), calls=%async_computation.2 | async-start | bytes 2064384 | tf_op jit(solution)/shard_map/reduce_scatter | solution.py:91
  154.1 18.0 %copy-start.4 = (bf16[3584]{0:T(1024)(128)(2,1)S(1)}, bf16[3584]{0:T(1024)(128)(2,1)}, u32[]{:S(2)}) copy-start(bf16[3584]{0:T(1024)(128)(2,1)} %param.18) | copy-start | bytes 21508
  154.1 86.7 %copy-start.1 = (bf16[64,896]{1,0:T(8,128)(2,1)S(1)}, bf16[64,896]{1,0:T(8,128)(2,1)}, u32[]{:S(2)}) copy-start(bf16[64,896]{1,0:T(8,128)(2,1)} %param.11) | copy-start | bytes 344068
Sparse Core Ops, SparseCore 0:
  77.7 33.7 all-reduce.1
  172.3 66.8 reduce-scatter.1
where the time goes:
time: 248 us
  waiting for transfers between devices  101 us (41%)
  blocking collectives  96 us (39%)
  matrix products  32.4 us (13%)
  between operations  13.5 us (5%)
  other arithmetic  4.87 us (2%)
    reduce_scatter x1, waiting for transfers between devices, per_device(): lax.psum_scatter(jnp.dot(rows, down_weight, preferred_element_type=jnp.fl...  66.8 us
    psum x1, waiting for transfers between devices, per_device(): total = lax.psum(projected.astype(jnp.bfloat16), 'tp').astype(jnp.float32)  33.9 us
    all_gather x1, blocking collectives, per_device(): piece = lax.all_gather(normed, 'ctx', axis=0, tiled=True)  32.6 us
    all_gather x1, blocking collectives, per_device(): key_piece = lax.all_gather(keys, 'ctx', axis=0, tiled=True)  32.6 us
    all_gather x1, blocking collectives, per_device(): value_piece = lax.all_gather(values, 'ctx', axis=0, tiled=True)  30.7 us
    dot_general x1, matrix products, per_device(): jnp.dot(rows, down_weight, preferred_element_type=jnp.float32)  18 us
    dot_general x1, matrix products, per_device(): gate_part = jnp.dot(piece, gate_weight, preferred_element_type=jnp.float32)  8.76 us
  transfers between devices with their start and end apart: 2, of which 2 were waited for; matrix products, arithmetic and copies ran while one was open for 0% of the time, Pallas kernels for 0%

commit v1 on v0

v1 whole, which is shorter than its diff:
```python
import functools

import jax
import jax.numpy as jnp
from jax import lax
from jax.experimental import pallas as pl
from jax.experimental.pallas import tpu as pltpu
from jax.sharding import PartitionSpec as P

HEADS = 28
KV_HEADS = 4
HEAD_DIM = 128
GROUP = HEADS // KV_HEADS
WIDTH = 512
PROJ = 1792
DOWN_SLOTS = 4
MESH = pl.DeviceIdType.MESH


def each(first, last, body):
    if last - first <= 4:
        for index in range(first, last):
            body(index)
    else:
        lax.fori_loop(first, last, lambda i, c: (body(i), c)[1], 0)


def loop(count, body):
    lax.fori_loop(0, count, lambda i, c: (body(i), c)[1], 0)


def kernel(
    ctx_count,
    tp_count,
    queries,
    keys,
    values,
    block_table,
    residual,
    out_weight,
    vectors,
    gate_weight,
    up_weight,
    down_weight,
    out,
    q_buf,
    kv_buf,
    heads_buf,
    res_buf,
    vec_buf,
    wo,
    wg,
    wu,
    wd,
    x,
    gate_acc,
    up_acc,
    hidden,
    p_send,
    p_recv,
    p_send2,
    p_recv2,
    p_sum,
    attended,
    d_send,
    d_recv,
    d_send2,
    d_recv2,
    d_sum,
    sem_q,
    sem_small,
    sem_wo,
    sem_wg,
    sem_wu,
    sem_wd,
    kv_zs,
    kv_zr,
    kv_ys,
    kv_yr,
    x_zs,
    x_zr,
    x_ys,
    x_yr,
    p_s1,
    p_r1,
    p_s2,
    p_r2,
    d_s1,
    d_r1,
    d_s2,
    d_r2,
):
    far = ctx_count // 2
    wide = tp_count // 2
    me = lax.axis_index("ctx")
    tp = lax.axis_index("tp")
    a, b = me // 2, me % 2
    e, f = tp // 2, tp % 2
    tokens = q_buf.shape[0] * q_buf.shape[1] * q_buf.shape[2]
    quarter = q_buf.shape[2]
    half = tokens // 2
    pieces = x.shape[0]
    proj_pieces = wo.shape[0]
    slots = wd.shape[0]
    width = x.shape[-1]

    def at_a(other):
        return (other * 2 + b, tp)

    beside = (a * 2 + (1 - b), tp)

    def at_e(other):
        return (me, other * 2 + f)

    core = (me, e * 2 + (1 - f))

    def q_copy(rel, i):
        row = pl.multiple_of((i * 2 + (f if rel == 0 else 1 - f)) * quarter, quarter)
        return pltpu.make_async_copy(
            queries.at[pl.ds(row, quarter), :], q_buf.at[rel, i], sem_q.at[rel, i]
        )

    def small_copies():
        return (
            pltpu.make_async_copy(keys, kv_buf.at[0, 0, a], sem_small.at[0]),
            pltpu.make_async_copy(values, kv_buf.at[1, 0, a], sem_small.at[1]),
            pltpu.make_async_copy(residual, res_buf, sem_small.at[2]),
            pltpu.make_async_copy(vectors, vec_buf, sem_small.at[3]),
        )

    def wo_copy(n):
        column = pl.multiple_of(n * wo.shape[2], 128)
        return pltpu.make_async_copy(
            out_weight.at[:, pl.ds(column, wo.shape[2])], wo.at[n], sem_wo.at[n]
        )

    def wg_copy(k):
        row = pl.multiple_of(k * width, width)
        return pltpu.make_async_copy(
            gate_weight.at[pl.ds(row, width), :], wg.at[k], sem_wg.at[k]
        )

    def wu_copy(k):
        row = pl.multiple_of(k * width, width)
        return pltpu.make_async_copy(
            up_weight.at[pl.ds(row, width), :], wu.at[k], sem_wu.at[k]
        )

    def wd_copy(n):
        column = pl.multiple_of(n * width, width)
        return pltpu.make_async_copy(
            down_weight.at[:, pl.ds(column, width)], wd.at[n % slots], sem_wd.at[n]
        )

    for copy in small_copies():
        copy.start()
    for rel in range(2):
        for i in range(wide):
            q_copy(rel, i).start()
    for n in range(proj_pieces):
        wo_copy(n).start()

    def start_pair(k):
        wg_copy(k).start()
        wu_copy(k).start()

    loop(pieces, start_pair)
    loop(slots, lambda n: wd_copy(n).start())

    barrier = pltpu.get_barrier_semaphore()

    def greet(device):
        pl.semaphore_signal(barrier, inc=1, device_id=device, device_id_type=MESH)

    greet(beside)
    greet(core)
    each(1, far, lambda i: greet(at_a(lax.rem(a + i, far))))
    each(1, wide, lambda i: greet(at_e(lax.rem(e + i, wide))))
    pl.semaphore_wait(barrier, 2 + far - 1 + wide - 1)

    def remote(src, dst, send, recv, device):
        return pltpu.make_async_remote_copy(
            src_ref=src,
            dst_ref=dst,
            send_sem=send,
            recv_sem=recv,
            device_id=device,
            device_id_type=MESH,
        )

    def kv_far(w, i):
        return remote(
            kv_buf.at[w, 0, a],
            kv_buf.at[w, 0, a],
            kv_zs.at[w, i],
            kv_zr.at[w, a],
            at_a(lax.rem(a + i, far)),
        )

    def kv_from(w, source):
        return remote(
            kv_buf.at[w, 0, source],
            kv_buf.at[w, 0, source],
            kv_zs.at[w, 0],
            kv_zr.at[w, source],
            beside,
        )

    def kv_beside(w, source):
        return remote(
            kv_buf.at[w, 0, source],
            kv_buf.at[w, 1, source],
            kv_ys.at[w, source],
            kv_yr.at[w, source],
            beside,
        )

    for w in range(2):
        small_copies()[w].wait()
        each(1, far, lambda i, w=w: kv_far(w, i).start())
        kv_beside(w, a).start()

    key_count = 2 * far * tokens
    row = lax.broadcasted_iota(jnp.int32, (1, key_count), 1)
    slot = row // tokens
    local = row % tokens

    def place_slot(c, pair):
        owner = (c % far) * 2 + lax.rem(b + c // far, 2)
        return jnp.where(slot == c, block_table[owner], pair)

    pair = lax.fori_loop(
        0, 2 * far, place_slot, jnp.zeros((1, key_count), jnp.int32)
    )
    mirror = 2 * ctx_count - 1
    key_place = jnp.where(
        local < half, pair * half + local, (mirror - pair) * half + local - half
    )
    q_row = lax.broadcasted_iota(jnp.int32, (tokens, 1), 0)
    q_block = q_row // quarter
    q_core = jnp.where(q_block < wide, f, 1 - f)
    q_local = ((q_block % wide) * 2 + q_core) * quarter + q_row % quarter
    own = block_table[me]
    q_place = jnp.where(
        q_local < half, own * half + q_local, (mirror - own) * half + q_local - half
    )
    gate_acc[...] = jnp.zeros_like(gate_acc)
    up_acc[...] = jnp.zeros_like(up_acc)

    def kv_pass(i):
        source = lax.rem(a + i, far)
        for w in range(2):
            kv_from(w, source).wait_recv()
            kv_beside(w, source).start()

    each(1, far, kv_pass)
    for rel in range(2):
        for i in range(wide):
            q_copy(rel, i).wait()

    def kv_arrived(source):
        for w in range(2):
            kv_beside(w, source).wait_recv()

    each(0, far, kv_arrived)

    visible = key_place <= q_place
    all_keys = kv_buf[0].reshape(key_count, HEAD_DIM)
    all_values = kv_buf[1].reshape(key_count, HEAD_DIM)
    for head in range(GROUP):
        lanes = slice(head * HEAD_DIM, (head + 1) * HEAD_DIM)
        q_head = q_buf[:, :, :, lanes].reshape(tokens, HEAD_DIM)
        score = lax.dot_general(
            q_head,
            all_keys,
            (((1,), (1,)), ((), ())),
            preferred_element_type=jnp.float32,
        ) * (HEAD_DIM**-0.5)
        score = jnp.where(visible, score, -1e30)
        top = jnp.max(score, axis=-1, keepdims=True)
        weight = jnp.where(visible, jnp.exp(score - top), 0.0)
        total = jnp.sum(weight, axis=-1, keepdims=True)
        added = jnp.dot(
            weight.astype(jnp.bfloat16), all_values, preferred_element_type=jnp.float32
        )
        heads_buf[:, lanes] = (added / total).astype(jnp.bfloat16)

    def p_core(n):
        return remote(p_send.at[n], p_recv.at[n], p_s1.at[n], p_r1.at[n], core)

    def p_wide(n, i):
        other = lax.rem(e + i, wide)
        return remote(
            p_send2.at[n, other],
            p_recv2.at[n, e],
            p_s2.at[n, other],
            p_r2.at[n, e],
            at_e(other),
        )

    def p_from(n, source):
        return remote(
            p_send2.at[n, source],
            p_recv2.at[n, source],
            p_s2.at[n, source],
            p_r2.at[n, source],
            at_e(source),
        )

    def p_step(n):
        wo_copy(n).wait()
        part = jnp.dot(heads_buf[...], wo[n], preferred_element_type=jnp.float32)
        part = part.reshape(2, wide, quarter, part.shape[-1])
        p_send[n] = part[1].astype(jnp.bfloat16)
        p_core(n).start()
        p_sum[n] = part[0]

    def p_on(n):
        p_core(n).wait_recv()
        summed = p_sum[n] + p_recv[n].astype(jnp.float32)
        p_sum[n] = summed
        p_send2[n] = summed.astype(jnp.bfloat16)
        each(1, wide, lambda i: p_wide(n, i).start())

    for n in range(proj_pieces):
        p_step(n)
    for n in range(proj_pieces):
        p_on(n)
    for copy in small_copies()[2:]:
        copy.wait()
    square = jnp.zeros((quarter, 1), jnp.float32)
    for n in range(proj_pieces):
        cols = slice(n * wo.shape[2], (n + 1) * wo.shape[2])
        head_sum = p_sum[n, e]
        for i in range(1, wide):
            source = lax.rem(e + i, wide)
            p_from(n, source).wait_recv()
            head_sum = head_sum + p_recv2[n, source].astype(jnp.float32)
        att = (res_buf[:, cols].astype(jnp.float32) + head_sum).astype(jnp.bfloat16)
        att = att.astype(jnp.float32)
        attended[:, cols] = att
        square = square + jnp.sum(att * att, axis=-1, keepdims=True)
    depth = proj_pieces * wo.shape[2]
    inverse = lax.rsqrt(square / depth + 1e-6)

    def x_far(k, i):
        return remote(
            x.at[k, 0, a],
            x.at[k, 0, a],
            x_zs.at[k, i],
            x_zr.at[k, a],
            at_a(lax.rem(a + i, far)),
        )

    def x_from(k, source):
        return remote(
            x.at[k, 0, source],
            x.at[k, 0, source],
            x_zs.at[k, 0],
            x_zr.at[k, source],
            beside,
        )

    def x_beside(k, source):
        return remote(
            x.at[k, 0, source],
            x.at[k, 1, source],
            x_ys.at[k, source],
            x_yr.at[k, source],
            beside,
        )

    logit = jnp.zeros((quarter, 1), jnp.float32)
    for k in range(pieces):
        cols = slice(k * width, (k + 1) * width)
        normed = (attended[:, cols] * inverse * vec_buf[0:1, cols]).astype(jnp.bfloat16)
        x[k, 0, a] = normed
        each(1, far, lambda i, k=k: x_far(k, i).start())
        x_beside(k, a).start()
        logit = logit + jnp.sum(
            normed.astype(jnp.float32) * vec_buf[1:2, cols], axis=-1, keepdims=True
        )
    gate_prob = jax.nn.sigmoid(logit)

    def x_pass(k):
        def one(i):
            source = lax.rem(a + i, far)
            x_from(k, source).wait_recv()
            x_beside(k, source).start()

        each(1, far, one)

    rows = 2 * far * quarter

    def expand(k):
        @pl.when(k + 1 < pieces)
        def _():
            x_pass(k + 1)

        wg_copy(k).wait()
        wu_copy(k).wait()
        each(0, far, lambda source: x_beside(k, source).wait_recv())
        piece = x[k].reshape(rows, width)
        gate_acc[...] += jnp.dot(piece, wg[k], preferred_element_type=jnp.float32)
        up_acc[...] += jnp.dot(piece, wu[k], preferred_element_type=jnp.float32)

    x_pass(0)
    loop(pieces, expand)
    gate = gate_acc[...]
    hidden[...] = (gate / (1.0 + jnp.exp(-gate)) * up_acc[...]).astype(jnp.bfloat16)

    def d_beside(n):
        return remote(d_send.at[n], d_recv.at[n], d_s1.at[n], d_r1.at[n], beside)

    def d_far(n, i):
        other = lax.rem(a + i, far)
        return remote(
            d_send2.at[n, other],
            d_recv2.at[n, a],
            d_s2.at[n, other],
            d_r2.at[n, a],
            at_a(other),
        )

    def d_from(n, source):
        return remote(
            d_send2.at[n, source],
            d_recv2.at[n, source],
            d_s2.at[n, source],
            d_r2.at[n, source],
            at_a(source),
        )

    def d_on(n):
        d_beside(n).wait_recv()
        summed = d_sum[n] + d_recv[n].astype(jnp.float32)
        d_sum[n] = summed
        d_send2[n] = summed.astype(jnp.bfloat16)
        each(1, far, lambda i: d_far(n, i).start())

    def contract(n):
        wd_copy(n).wait()
        part = jnp.dot(hidden[...], wd[n % slots], preferred_element_type=jnp.float32)
        part = part.reshape(2, far, quarter, width)
        d_send[n] = part[1].astype(jnp.bfloat16)
        d_beside(n).start()
        d_sum[n] = part[0]

        @pl.when(n + slots < pieces)
        def _():
            wd_copy(n + slots).start()

        @pl.when(n > 0)
        def _():
            d_on(n - 1)

    loop(pieces, contract)
    d_on(pieces - 1)
    for n in range(pieces):
        cols = slice(n * width, (n + 1) * width)
        shared = d_sum[n, a]

        def add(i, shared, n=n):
            source = lax.rem(a + i, far)
            d_from(n, source).wait_recv()
            return shared + d_recv2[n, source].astype(jnp.float32)

        if far <= 4:
            for i in range(1, far):
                shared = add(i, shared)
        else:
            shared = lax.fori_loop(1, far, add, shared)
        out[:, cols] = (attended[:, cols] + gate_prob * shared).astype(jnp.bfloat16)

    for w in range(2):
        each(1, far, lambda i, w=w: kv_far(w, i).wait_send())
        each(0, far, lambda source, w=w: kv_beside(w, source).wait_send())
    for n in range(proj_pieces):
        p_core(n).wait_send()
        each(1, wide, lambda i, n=n: p_wide(n, i).wait_send())

    def drain(k):
        each(1, far, lambda i: x_far(k, i).wait_send())
        each(0, far, lambda source: x_beside(k, source).wait_send())
        d_beside(k).wait_send()
        each(1, far, lambda i: d_far(k, i).wait_send())

    loop(pieces, drain)


def per_device(
    queries,
    keys,
    values,
    block_table,
    residual,
    out_weight,
    norm_gain,
    gate_logit_weight,
    gate_weight,
    up_weight,
    down_weight,
):
    tokens = queries.shape[0]
    ctx_count = lax.axis_size("ctx")
    tp_count = lax.axis_size("tp")
    far, wide = ctx_count // 2, tp_count // 2
    quarter, depth = residual.shape
    units = gate_weight.shape[1]
    pieces = depth // WIDTH
    proj_pieces = depth // PROJ
    slots = min(DOWN_SLOTS, pieces)
    rows = ctx_count * quarter
    vectors = jnp.stack([norm_gain, gate_logit_weight]).astype(jnp.float32)
    bf16, f32 = jnp.bfloat16, jnp.float32
    dma = pltpu.SemaphoreType.DMA
    any_space = pl.BlockSpec(memory_space=pl.ANY)
    matmul = rows * depth * units * 3 + tokens * queries.shape[1] * depth
    return pl.pallas_call(
        functools.partial(kernel, ctx_count, tp_count),
        out_shape=jax.ShapeDtypeStruct((quarter, depth), bf16),
        in_specs=[any_space] * 3
        + [pl.BlockSpec(memory_space=pltpu.SMEM)]
        + [any_space] * 6,
        out_specs=pl.BlockSpec(memory_space=pltpu.VMEM),
        scratch_shapes=[
            pltpu.VMEM((2, wide, quarter, queries.shape[1]), bf16),
            pltpu.VMEM((2, 2, far, tokens, HEAD_DIM), bf16),
            pltpu.VMEM((tokens, queries.shape[1]), bf16),
            pltpu.VMEM((quarter, depth), bf16),
            pltpu.VMEM((2, depth), f32),
            pltpu.VMEM((proj_pieces, out_weight.shape[0], PROJ), bf16),
            pltpu.VMEM((pieces, WIDTH, units), bf16),
            pltpu.VMEM((pieces, WIDTH, units), bf16),
            pltpu.VMEM((slots, units, WIDTH), bf16),
            pltpu.VMEM((pieces, 2, far, quarter, WIDTH), bf16),
            pltpu.VMEM((rows, units), f32),
            pltpu.VMEM((rows, units), f32),
            pltpu.VMEM((rows, units), bf16),
            pltpu.VMEM((proj_pieces, wide, quarter, PROJ), bf16),
            pltpu.VMEM((proj_pieces, wide, quarter, PROJ), bf16),
            pltpu.VMEM((proj_pieces, wide, quarter, PROJ), bf16),
            pltpu.VMEM((proj_pieces, wide, quarter, PROJ), bf16),
            pltpu.VMEM((proj_pieces, wide, quarter, PROJ), f32),
            pltpu.VMEM((quarter, depth), f32),
            pltpu.VMEM((pieces, far, quarter, WIDTH), bf16),
            pltpu.VMEM((pieces, far, quarter, WIDTH), bf16),
            pltpu.VMEM((pieces, far, quarter, WIDTH), bf16),
            pltpu.VMEM((pieces, far, quarter, WIDTH), bf16),
            pltpu.VMEM((pieces, far, quarter, WIDTH), f32),
            dma((2, wide)),
            dma((4,)),
            dma((proj_pieces,)),
            dma((pieces,)),
            dma((pieces,)),
            dma((pieces,)),
            dma((2, far)),
            dma((2, far)),
            dma((2, far)),
            dma((2, far)),
            dma((pieces, far)),
            dma((pieces, far)),
            dma((pieces, far)),
            dma((pieces, far)),
            dma((proj_pieces,)),
            dma((proj_pieces,)),
            dma((proj_pieces, wide)),
            dma((proj_pieces, wide)),
            dma((pieces,)),
            dma((pieces,)),
            dma((pieces, far)),
            dma((pieces, far)),
        ],
        compiler_params=pltpu.CompilerParams(
            collective_id=0,
            has_side_effects=True,
            vmem_limit_bytes=63 * 1024 * 1024,
        ),
        cost_estimate=pl.CostEstimate(
            flops=2 * matmul,
            bytes_accessed=2 * (3 * depth * units + out_weight.size),
            transcendentals=rows * units,
        ),
        name="layer",
    )(
        queries,
        keys,
        values,
        block_table,
        residual,
        out_weight,
        vectors,
        gate_weight,
        up_weight,
        down_weight,
    )


def solution(mesh):
    return jax.shard_map(
        per_device,
        mesh=mesh,
        in_specs=(
            P("ctx", "tp"),
            P("ctx", "tp"),
            P("ctx", "tp"),
            P(),
            P(("ctx", "tp"), None),
            P("tp", None),
            P(),
            P(),
            P(None, "ctx"),
            P(None, "ctx"),
            P("ctx", None),
        ),
        out_specs=P(("ctx", "tp"), None),
        check_vma=False,
    )
```

time: 248 us -> 70.3 us (0.28)
  waiting for transfers between devices: 101 us -> 0 us
  blocking collectives: 96 us -> 0 us
  Pallas kernels: 0 us -> 66.4 us
  matrix products: 32.4 us -> 0 us
  between operations: 13.5 us -> 0.02 us
  other arithmetic: 4.87 us -> 0.65 us
  local copies, waits for them, and re-layouts: 0.12 us -> 2.97 us
    all_gather x3 -> x0, blocking collectives: 96 us -> none  [the longest x1 32.6 us: per_device(): piece = lax.all_gather(normed, 'ctx', axis=0, tiled=True)]
    reduce_scatter x1 -> x0, waiting for transfers between devices: 66.8 us -> none  [per_device(): lax.psum_scatter(jnp.dot(rows, down_weight, preferred_element_type=jnp.fl...]
    pallas_call x0 -> x1, Pallas kernels: none -> 66.4 us  [per_device(): pl.pallas_call(functools.partial(kernel, ctx_count, tp_count), out_shape=...]
    psum x1 -> x0, waiting for transfers between devices: 33.9 us -> none  [per_device(): total = lax.psum(projected.astype(jnp.bfloat16), 'tp').astype(jnp.float32)]
    dot_general x6 -> x0, matrix products: 32.4 us -> none  [the longest x1 18 us: per_device(): jnp.dot(rows, down_weight, preferred_element_type=jnp.float32)]
  transfers between devices with their start and end apart: 2 -> 0, of which waited for: 2 -> 0; matrix products, arithmetic and copies ran while one was open for 0% -> 0% of each run, Pallas kernels for 0% -> 0%
where the time goes in v1:
time: 70.3 us; the launch traced here: 70 us
  Pallas kernels  66.4 us (94%)
  local copies, waits for them, and re-layouts  2.97 us (4%)
    pallas_call x1, Pallas kernels, per_device(): pl.pallas_call(functools.partial(kernel, ctx_count, tp_count), out_shape=...  66.4 us
    unnamed x1, local copies, waits for them, and re-layouts  1.55 us
    another operation x2, local copies, waits for them, and re-layouts, per_device(): vectors = jnp.stack([norm_gain, gate_logit_weight]).astype(jnp.float32)  1.41 us

profile of v1, /device:TPU:0, one launch (start us, length us, event | category | flops | bytes accessed | tf_op | source)
XLA Modules:
  0.0 70.0 jit_solution(9796644090345487448)
XLA Ops:
  0.0 0.7 %stack.9 = bf16[1,3584]{1,0:T(2,128)(2,1)S(1)} reshape(bf16[3584]{0:T(1024)(128)(2,1)} %param.17) | data formatting | bytes 14336 | tf_op jit(solution)/shard_map/stack | solution.py:514
  0.7 0.7 %stack.10 = bf16[1,3584]{1,0:T(2,128)(2,1)S(1)} reshape(bf16[3584]{0:T(1024)(128)(2,1)} %param.18) | data formatting | bytes 14336 | tf_op jit(solution)/shard_map/stack | solution.py:514
  1.4 0.6 maximum_convert_fusion.vectors
  2.1 66.4 %layer.1 = bf16[16,3584]{1,0:T(8,128)(2,1)} custom-call(bf16[64,896]{1,0:T(8,128)(2,1)} %queries.1, bf16[64,128]{1,0:T(8,128)(2,1)} %keys.1, bf16[64,128]{1,0:T(8,128)(2,1)} %values.1, s32[8]{0:T(128)} %block_table.1, bf16[16,3584]{1,0:T(8,128)(2,1)} %residual.1, bf16[896,3584]{1,0:T(8,128)(2,1)} %out_weight.1, f32[2,3584]{1,0:T(2,128)} %maximum_convert_fusion.vectors, ...), custom_call_target="tpu_custom_call" | custom-call | flops 7457472512 | bytes 61472768 | tf_op jit(solution)/shard_map/layer/pallas_call | solution.py:519
  68.5 1.6 %copy.13 = bf16[16,3584]{1,0:T(8,128)(2,1)} copy(bf16[16,3584]{1,0:T(8,128)(2,1)} %layer.1) | data formatting | bytes 229376

commit v2 on v1

--- a/solution.py
+++ b/solution.py
@@ -14,6 +14,8 @@
 WIDTH = 512
 PROJ = 1792
 DOWN_SLOTS = 4
+AHEAD = 2
+BEHIND = 3
 MESH = pl.DeviceIdType.MESH
 
 
@@ -38,7 +40,8 @@
     block_table,
     residual,
     out_weight,
-    vectors,
+    norm_gain,
+    logit_weight,
     gate_weight,
     up_weight,
     down_weight,
@@ -47,7 +50,8 @@
     kv_buf,
     heads_buf,
     res_buf,
-    vec_buf,
+    gain_buf,
+    logit_buf,
     wo,
     wg,
     wu,
@@ -125,7 +129,8 @@
             pltpu.make_async_copy(keys, kv_buf.at[0, 0, a], sem_small.at[0]),
             pltpu.make_async_copy(values, kv_buf.at[1, 0, a], sem_small.at[1]),
             pltpu.make_async_copy(residual, res_buf, sem_small.at[2]),
-            pltpu.make_async_copy(vectors, vec_buf, sem_small.at[3]),
+            pltpu.make_async_copy(norm_gain, gain_buf, sem_small.at[3]),
+            pltpu.make_async_copy(logit_weight, logit_buf, sem_small.at[4]),
         )
 
     def wo_copy(n):
@@ -373,12 +378,12 @@
     logit = jnp.zeros((quarter, 1), jnp.float32)
     for k in range(pieces):
         cols = slice(k * width, (k + 1) * width)
-        normed = (attended[:, cols] * inverse * vec_buf[0:1, cols]).astype(jnp.bfloat16)
+        normed = (attended[:, cols] * inverse * gain_buf[cols].astype(jnp.float32).reshape(1, width)).astype(jnp.bfloat16)
         x[k, 0, a] = normed
         each(1, far, lambda i, k=k: x_far(k, i).start())
         x_beside(k, a).start()
         logit = logit + jnp.sum(
-            normed.astype(jnp.float32) * vec_buf[1:2, cols], axis=-1, keepdims=True
+            normed.astype(jnp.float32) * logit_buf[cols].astype(jnp.float32).reshape(1, width), axis=-1, keepdims=True
         )
     gate_prob = jax.nn.sigmoid(logit)
 
@@ -393,9 +398,9 @@
     rows = 2 * far * quarter
 
     def expand(k):
-        @pl.when(k + 1 < pieces)
+        @pl.when(k + AHEAD < pieces)
         def _():
-            x_pass(k + 1)
+            x_pass(k + AHEAD)
 
         wg_copy(k).wait()
         wu_copy(k).wait()
@@ -404,7 +409,8 @@
         gate_acc[...] += jnp.dot(piece, wg[k], preferred_element_type=jnp.float32)
         up_acc[...] += jnp.dot(piece, wu[k], preferred_element_type=jnp.float32)
 
-    x_pass(0)
+    for k in range(min(AHEAD, pieces)):
+        x_pass(k)
     loop(pieces, expand)
     gate = gate_acc[...]
     hidden[...] = (gate / (1.0 + jnp.exp(-gate)) * up_acc[...]).astype(jnp.bfloat16)
@@ -450,12 +456,13 @@
         def _():
             wd_copy(n + slots).start()
 
-        @pl.when(n > 0)
+        @pl.when(n >= BEHIND)
         def _():
-            d_on(n - 1)
+            d_on(n - BEHIND)
 
     loop(pieces, contract)
-    d_on(pieces - 1)
+    for n in range(max(pieces - BEHIND, 0), pieces):
+        d_on(n)
     for n in range(pieces):
         cols = slice(n * width, (n + 1) * width)
         shared = d_sum[n, a]
@@ -470,7 +477,7 @@
                 shared = add(i, shared)
         else:
             shared = lax.fori_loop(1, far, add, shared)
-        out[:, cols] = (attended[:, cols] + gate_prob * shared).astype(jnp.bfloat16)
+        out[:, cols] = attended[:, cols] + gate_prob * shared
 
     for w in range(2):
         each(1, far, lambda i, w=w: kv_far(w, i).wait_send())
@@ -511,24 +518,24 @@
     proj_pieces = depth // PROJ
     slots = min(DOWN_SLOTS, pieces)
     rows = ctx_count * quarter
-    vectors = jnp.stack([norm_gain, gate_logit_weight]).astype(jnp.float32)
     bf16, f32 = jnp.bfloat16, jnp.float32
     dma = pltpu.SemaphoreType.DMA
     any_space = pl.BlockSpec(memory_space=pl.ANY)
     matmul = rows * depth * units * 3 + tokens * queries.shape[1] * depth
-    return pl.pallas_call(
+    layer_out = pl.pallas_call(
         functools.partial(kernel, ctx_count, tp_count),
-        out_shape=jax.ShapeDtypeStruct((quarter, depth), bf16),
+        out_shape=jax.ShapeDtypeStruct((quarter, depth), f32),
         in_specs=[any_space] * 3
         + [pl.BlockSpec(memory_space=pltpu.SMEM)]
-        + [any_space] * 6,
+        + [any_space] * 7,
         out_specs=pl.BlockSpec(memory_space=pltpu.VMEM),
         scratch_shapes=[
             pltpu.VMEM((2, wide, quarter, queries.shape[1]), bf16),
             pltpu.VMEM((2, 2, far, tokens, HEAD_DIM), bf16),
             pltpu.VMEM((tokens, queries.shape[1]), bf16),
             pltpu.VMEM((quarter, depth), bf16),
-            pltpu.VMEM((2, depth), f32),
+            pltpu.VMEM((depth,), bf16),
+            pltpu.VMEM((depth,), bf16),
             pltpu.VMEM((proj_pieces, out_weight.shape[0], PROJ), bf16),
             pltpu.VMEM((pieces, WIDTH, units), bf16),
             pltpu.VMEM((pieces, WIDTH, units), bf16),
@@ -549,7 +556,7 @@
             pltpu.VMEM((pieces, far, quarter, WIDTH), bf16),
             pltpu.VMEM((pieces, far, quarter, WIDTH), f32),
             dma((2, wide)),
-            dma((4,)),
+            dma((5,)),
             dma((proj_pieces,)),
             dma((pieces,)),
             dma((pieces,)),
@@ -589,11 +596,13 @@
         block_table,
         residual,
         out_weight,
-        vectors,
+        norm_gain,
+        gate_logit_weight,
         gate_weight,
         up_weight,
         down_weight,
     )
+    return layer_out.astype(bf16)
 
 
 def solution(mesh):

time: 70.3 us -> 60.3 us (0.86)
  Pallas kernels: 66.4 us -> 58.6 us
  local copies, waits for them, and re-layouts: 2.97 us -> 0 us
  other arithmetic: 0.65 us -> 1.6 us
    pallas_call x1, Pallas kernels: 66.4 us -> 58.6 us  [per_device(): pl.pallas_call(functools.partial(kernel, ctx_count, tp_count), out_shape=...]
    unnamed x1 -> x0, local copies, waits for them, and re-layouts: 1.55 us -> none
    another operation x2 -> x0, local copies, waits for them, and re-layouts: 1.41 us -> none  [per_device(): vectors = jnp.stack([norm_gain, gate_logit_weight]).astype(jnp.float32)]
    convert_element_type x1, other arithmetic: 0.65 us -> 1.6 us  [per_device(): return layer_out.astype(bf16)]
where the time goes in v2:
time: 60.3 us; the launch traced here: 60.2 us
  Pallas kernels  58.6 us (97%)
  other arithmetic  1.6 us (3%)
    pallas_call x1, Pallas kernels, per_device(): pl.pallas_call(functools.partial(kernel, ctx_count, tp_count), out_shape=...  58.6 us
    convert_element_type x1, other arithmetic, per_device(): return layer_out.astype(bf16)  1.6 us

profile of v2, /device:TPU:0, one launch (start us, length us, event | category | flops | bytes accessed | tf_op | source)
XLA Modules:
  0.0 60.2 jit_solution(7669746180131510545)
XLA Ops:
  0.0 58.6 %layer.1 = f32[16,3584]{1,0:T(8,128)} custom-call(bf16[64,896]{1,0:T(8,128)(2,1)} %queries.1, bf16[64,128]{1,0:T(8,128)(2,1)} %keys.1, bf16[64,128]{1,0:T(8,128)(2,1)} %values.1, s32[8]{0:T(128)} %block_table.1, bf16[16,3584]{1,0:T(8,128)(2,1)} %residual.1, bf16[896,3584]{1,0:T(8,128)(2,1)} %out_weight.1, bf16[3584]{0:T(1024)(128)(2,1)} %norm_gain.1, ...), custom_call_target="tpu_custom_call" | custom-call | flops 7457472512 | bytes 61472768 | tf_op jit(solution)/shard_map/layer/pallas_call | solution.py:525
  58.6 1.6 %convert_element_type.3 = bf16[16,3584]{1,0:T(8,128)(2,1)} convert(f32[16,3584]{1,0:T(8,128)} %layer.1) | non-fusion elementwise | flops 57344 | bytes 344064 | tf_op jit(solution)/shard_map/convert_element_type | solution.py:605

commit v3 on v2

--- a/solution.py
+++ b/solution.py
@@ -169,9 +169,6 @@
         wg_copy(k).start()
         wu_copy(k).start()
 
-    loop(pieces, start_pair)
-    loop(slots, lambda n: wd_copy(n).start())
-
     barrier = pltpu.get_barrier_semaphore()
 
     def greet(device):
@@ -224,6 +221,7 @@
         small_copies()[w].wait()
         each(1, far, lambda i, w=w: kv_far(w, i).start())
         kv_beside(w, a).start()
+    start_pair(0)
 
     key_count = 2 * far * tokens
     row = lax.broadcasted_iota(jnp.int32, (1, key_count), 1)
@@ -259,6 +257,8 @@
             kv_beside(w, source).start()
 
     each(1, far, kv_pass)
+    start_pair(1)
+    start_pair(2)
     for rel in range(2):
         for i in range(wide):
             q_copy(rel, i).wait()
@@ -269,6 +269,7 @@
 
     each(0, far, kv_arrived)
 
+    start_pair(3)
     visible = key_place <= q_place
     all_keys = kv_buf[0].reshape(key_count, HEAD_DIM)
     all_values = kv_buf[1].reshape(key_count, HEAD_DIM)
@@ -331,6 +332,7 @@
         p_step(n)
     for n in range(proj_pieces):
         p_on(n)
+    start_pair(4)
     for copy in small_copies()[2:]:
         copy.wait()
     square = jnp.zeros((quarter, 1), jnp.float32)
@@ -386,6 +388,7 @@
             normed.astype(jnp.float32) * logit_buf[cols].astype(jnp.float32).reshape(1, width), axis=-1, keepdims=True
         )
     gate_prob = jax.nn.sigmoid(logit)
+    start_pair(5)
 
     def x_pass(k):
         def one(i):
@@ -401,6 +404,14 @@
         @pl.when(k + AHEAD < pieces)
         def _():
             x_pass(k + AHEAD)
+
+        @pl.when(k + 6 < pieces)
+        def _():
+            start_pair(k + 6)
+
+        @pl.when((k >= 1) & (k <= slots))
+        def _():
+            wd_copy(k - 1).start()
 
         wg_copy(k).wait()
         wu_copy(k).wait()

time: 60.3 us -> 60.2 us (level)
  no operation moved by 1% of the time
where the time goes in v3:
time: 60.2 us; the launch traced here: 60.1 us
  Pallas kernels  58.5 us (97%)
  other arithmetic  1.6 us (3%)
    pallas_call x1, Pallas kernels, per_device(): pl.pallas_call(functools.partial(kernel, ctx_count, tp_count), out_shape=...  58.5 us
    convert_element_type x1, other arithmetic, per_device(): return layer_out.astype(bf16)  1.6 us

profile of v3, /device:TPU:0, one launch (start us, length us, event | category | flops | bytes accessed | tf_op | source)
XLA Modules:
  0.0 60.1 jit_solution(15151617184877844551)
XLA Ops:
  0.0 58.5 %layer.1 = f32[16,3584]{1,0:T(8,128)} custom-call(bf16[64,896]{1,0:T(8,128)(2,1)} %queries.1, bf16[64,128]{1,0:T(8,128)(2,1)} %keys.1, bf16[64,128]{1,0:T(8,128)(2,1)} %values.1, s32[8]{0:T(128)} %block_table.1, bf16[16,3584]{1,0:T(8,128)(2,1)} %residual.1, bf16[896,3584]{1,0:T(8,128)(2,1)} %out_weight.1, bf16[3584]{0:T(1024)(128)(2,1)} %norm_gain.1, ...), custom_call_target="tpu_custom_call" | custom-call | flops 7457472512 | bytes 61472768 | tf_op jit(solution)/shard_map/layer/pallas_call | solution.py:536
  58.5 1.6 %convert_element_type.3 = bf16[16,3584]{1,0:T(8,128)(2,1)} convert(f32[16,3584]{1,0:T(8,128)} %layer.1) | non-fusion elementwise | flops 57344 | bytes 344064 | tf_op jit(solution)/shard_map/convert_element_type | solution.py:616

commit v4 on v3

--- a/solution.py
+++ b/solution.py
@@ -12,8 +12,8 @@
 HEAD_DIM = 128
 GROUP = HEADS // KV_HEADS
 WIDTH = 512
-PROJ = 1792
-DOWN_SLOTS = 4
+PROJ = WIDTH
+DOWN_SLOTS = 3
 AHEAD = 2
 BEHIND = 3
 MESH = pl.DeviceIdType.MESH
@@ -93,6 +93,11 @@
     d_r1,
     d_s2,
     d_r2,
+    inv_buf,
+    inv_zs,
+    inv_zr,
+    inv_ys,
+    inv_yr,
 ):
     far = ctx_count // 2
     wide = tp_count // 2
@@ -328,16 +333,75 @@
         p_send2[n] = summed.astype(jnp.bfloat16)
         each(1, wide, lambda i: p_wide(n, i).start())
 
-    for n in range(proj_pieces):
-        p_step(n)
-    for n in range(proj_pieces):
-        p_on(n)
-    start_pair(4)
-    for copy in small_copies()[2:]:
-        copy.wait()
-    square = jnp.zeros((quarter, 1), jnp.float32)
-    for n in range(proj_pieces):
-        cols = slice(n * wo.shape[2], (n + 1) * wo.shape[2])
+    def x_far(k, i):
+        return remote(
+            x.at[k, 0, a],
+            x.at[k, 0, a],
+            x_zs.at[k, i],
+            x_zr.at[k, a],
+            at_a(lax.rem(a + i, far)),
+        )
+
+    def x_from(k, source):
+        return remote(
+            x.at[k, 0, source],
+            x.at[k, 0, source],
+            x_zs.at[k, 0],
+            x_zr.at[k, source],
+            beside,
+        )
+
+    def x_beside(k, source):
+        return remote(
+            x.at[k, 0, source],
+            x.at[k, 1, source],
+            x_ys.at[k, source],
+            x_yr.at[k, source],
+            beside,
+        )
+
+    def x_pass(k):
+        def one(i):
+            source = lax.rem(a + i, far)
+            x_from(k, source).wait_recv()
+            x_beside(k, source).start()
+
+        each(1, far, one)
+
+    def inv_far(i):
+        return remote(
+            inv_buf.at[0, a],
+            inv_buf.at[0, a],
+            inv_zs.at[i],
+            inv_zr.at[a],
+            at_a(lax.rem(a + i, far)),
+        )
+
+    def inv_from(source):
+        return remote(
+            inv_buf.at[0, source],
+            inv_buf.at[0, source],
+            inv_zs.at[0],
+            inv_zr.at[source],
+            beside,
+        )
+
+    def inv_beside(source):
+        return remote(
+            inv_buf.at[0, source],
+            inv_buf.at[1, source],
+            inv_ys.at[source],
+            inv_yr.at[source],
+            beside,
+        )
+
+    def inv_pass(i):
+        source = lax.rem(a + i, far)
+        inv_from(source).wait_recv()
+        inv_beside(source).start()
+
+    def p_end(n, square):
+        cols = slice(n * width, (n + 1) * width)
         head_sum = p_sum[n, e]
         for i in range(1, wide):
             source = lax.rem(e + i, wide)
@@ -346,57 +410,31 @@
         att = (res_buf[:, cols].astype(jnp.float32) + head_sum).astype(jnp.bfloat16)
         att = att.astype(jnp.float32)
         attended[:, cols] = att
-        square = square + jnp.sum(att * att, axis=-1, keepdims=True)
-    depth = proj_pieces * wo.shape[2]
-    inverse = lax.rsqrt(square / depth + 1e-6)
-
-    def x_far(k, i):
-        return remote(
-            x.at[k, 0, a],
-            x.at[k, 0, a],
-            x_zs.at[k, i],
-            x_zr.at[k, a],
-            at_a(lax.rem(a + i, far)),
-        )
-
-    def x_from(k, source):
-        return remote(
-            x.at[k, 0, source],
-            x.at[k, 0, source],
-            x_zs.at[k, 0],
-            x_zr.at[k, source],
-            beside,
-        )
-
-    def x_beside(k, source):
-        return remote(
-            x.at[k, 0, source],
-            x.at[k, 1, source],
-            x_ys.at[k, source],
-            x_yr.at[k, source],
-            beside,
-        )
-
-    logit = jnp.zeros((quarter, 1), jnp.float32)
-    for k in range(pieces):
-        cols = slice(k * width, (k + 1) * width)
-        normed = (attended[:, cols] * inverse * gain_buf[cols].astype(jnp.float32).reshape(1, width)).astype(jnp.bfloat16)
-        x[k, 0, a] = normed
-        each(1, far, lambda i, k=k: x_far(k, i).start())
-        x_beside(k, a).start()
-        logit = logit + jnp.sum(
-            normed.astype(jnp.float32) * logit_buf[cols].astype(jnp.float32).reshape(1, width), axis=-1, keepdims=True
-        )
-    gate_prob = jax.nn.sigmoid(logit)
+        gain = gain_buf[cols].astype(jnp.float32).reshape(1, width)
+        x[n, 0, a] = (att * gain).astype(jnp.bfloat16)
+        each(1, far, lambda i: x_far(n, i).start())
+        x_beside(n, a).start()
+        return square + jnp.sum(att * att, axis=-1, keepdims=True)
+
+    for copy in small_copies()[2:]:
+        copy.wait()
+    square = jnp.zeros((quarter, 1), jnp.float32)
+    for step in range(pieces + 7):
+        if step < pieces:
+            p_step(step)
+        if 0 <= step - 3 < pieces:
+            p_on(step - 3)
+        if 0 <= step - 7 < pieces:
+            square = p_end(step - 7, square)
+        if step == pieces:
+            start_pair(4)
+        if step >= pieces + 7 - AHEAD:
+            x_pass(step - (pieces + 7 - AHEAD))
+    inverse = lax.rsqrt(square / (pieces * width) + 1e-6)
+    inv_buf[0, a] = jnp.broadcast_to(inverse, inv_buf.shape[2:])
+    each(1, far, lambda i: inv_far(i).start())
+    inv_beside(a).start()
     start_pair(5)
-
-    def x_pass(k):
-        def one(i):
-            source = lax.rem(a + i, far)
-            x_from(k, source).wait_recv()
-            x_beside(k, source).start()
-
-        each(1, far, one)
 
     rows = 2 * far * quarter
 
@@ -404,6 +442,10 @@
         @pl.when(k + AHEAD < pieces)
         def _():
             x_pass(k + AHEAD)
+
+        @pl.when(k == 2)
+        def _():
+            each(1, far, inv_pass)
 
         @pl.when(k + 6 < pieces)
         def _():
@@ -420,11 +462,12 @@
         gate_acc[...] += jnp.dot(piece, wg[k], preferred_element_type=jnp.float32)
         up_acc[...] += jnp.dot(piece, wu[k], preferred_element_type=jnp.float32)
 
-    for k in range(min(AHEAD, pieces)):
-        x_pass(k)
     loop(pieces, expand)
-    gate = gate_acc[...]
-    hidden[...] = (gate / (1.0 + jnp.exp(-gate)) * up_acc[...]).astype(jnp.bfloat16)
+    each(0, far, lambda source: inv_beside(source).wait_recv())
+    scale = inv_buf[...].reshape(rows, inv_buf.shape[-1])[:, 0:1]
+    gate = gate_acc[...] * scale
+    up = up_acc[...] * scale
+    hidden[...] = (gate / (1.0 + jnp.exp(-gate)) * up).astype(jnp.bfloat16)
 
     def d_beside(n):
         return remote(d_send.at[n], d_recv.at[n], d_s1.at[n], d_r1.at[n], beside)
@@ -472,6 +515,16 @@
             d_on(n - BEHIND)
 
     loop(pieces, contract)
+    logit = jnp.zeros((quarter, 1), jnp.float32)
+    for n in range(pieces):
+        cols = slice(n * width, (n + 1) * width)
+        gain = gain_buf[cols].astype(jnp.float32).reshape(1, width)
+        normed = (attended[:, cols] * inverse * gain).astype(jnp.bfloat16)
+        logit_w = logit_buf[cols].astype(jnp.float32).reshape(1, width)
+        logit = logit + jnp.sum(
+            normed.astype(jnp.float32) * logit_w, axis=-1, keepdims=True
+        )
+    gate_prob = jax.nn.sigmoid(logit)
     for n in range(max(pieces - BEHIND, 0), pieces):
         d_on(n)
     for n in range(pieces):
@@ -504,6 +557,8 @@
         each(1, far, lambda i: d_far(k, i).wait_send())
 
     loop(pieces, drain)
+    each(1, far, lambda i: inv_far(i).wait_send())
+    each(0, far, lambda source: inv_beside(source).wait_send())
 
 
 def per_device(
@@ -588,6 +643,11 @@
             dma((pieces,)),
             dma((pieces, far)),
             dma((pieces, far)),
+            pltpu.VMEM((2, far, quarter, 128), f32),
+            dma((far,)),
+            dma((far,)),
+            dma((far,)),
+            dma((far,)),
         ],
         compiler_params=pltpu.CompilerParams(
             collective_id=0,

time: 60.2 us -> 59.4 us (0.987)
  Pallas kernels: 58.5 us -> 57.6 us
    pallas_call x1, Pallas kernels: 58.5 us -> 57.6 us  [per_device(): pl.pallas_call(functools.partial(kernel, ctx_count, tp_count), out_shape=...]
where the time goes in v4:
time: 59.4 us; the launch traced here: 59.2 us
  Pallas kernels  57.6 us (97%)
  other arithmetic  1.6 us (3%)
    pallas_call x1, Pallas kernels, per_device(): pl.pallas_call(functools.partial(kernel, ctx_count, tp_count), out_shape=...  57.6 us
    convert_element_type x1, other arithmetic, per_device(): return layer_out.astype(bf16)  1.6 us

profile of v4, /device:TPU:0, one launch (start us, length us, event | category | flops | bytes accessed | tf_op | source)
XLA Modules:
  0.0 59.2 jit_solution(2633669041709195882)
XLA Ops:
  0.0 57.6 %layer.1 = f32[16,3584]{1,0:T(8,128)} custom-call(bf16[64,896]{1,0:T(8,128)(2,1)} %queries.1, bf16[64,128]{1,0:T(8,128)(2,1)} %keys.1, bf16[64,128]{1,0:T(8,128)(2,1)} %values.1, s32[8]{0:T(128)} %block_table.1, bf16[16,3584]{1,0:T(8,128)(2,1)} %residual.1, bf16[896,3584]{1,0:T(8,128)(2,1)} %out_weight.1, bf16[3584]{0:T(1024)(128)(2,1)} %norm_gain.1, ...), custom_call_target="tpu_custom_call" | custom-call | flops 7457472512 | bytes 61472768 | tf_op jit(solution)/shard_map/layer/pallas_call | solution.py:591
  57.6 1.6 %convert_element_type.3 = bf16[16,3584]{1,0:T(8,128)(2,1)} convert(f32[16,3584]{1,0:T(8,128)} %layer.1) | non-fusion elementwise | flops 57344 | bytes 344064 | tf_op jit(solution)/shard_map/convert_element_type | solution.py:676

commit v5 on v4

--- a/solution.py
+++ b/solution.py
@@ -13,7 +13,8 @@
 GROUP = HEADS // KV_HEADS
 WIDTH = 512
 PROJ = WIDTH
-DOWN_SLOTS = 3
+TILE = 256
+DOWN_SLOTS = 4
 AHEAD = 2
 BEHIND = 3
 MESH = pl.DeviceIdType.MESH
@@ -174,6 +175,9 @@
         wg_copy(k).start()
         wu_copy(k).start()
 
+    loop(pieces, start_pair)
+    loop(slots, lambda n: wd_copy(n).start())
+
     barrier = pltpu.get_barrier_semaphore()
 
     def greet(device):
@@ -226,7 +230,6 @@
         small_copies()[w].wait()
         each(1, far, lambda i, w=w: kv_far(w, i).start())
         kv_beside(w, a).start()
-    start_pair(0)
 
     key_count = 2 * far * tokens
     row = lax.broadcasted_iota(jnp.int32, (1, key_count), 1)
@@ -262,8 +265,6 @@
             kv_beside(w, source).start()
 
     each(1, far, kv_pass)
-    start_pair(1)
-    start_pair(2)
     for rel in range(2):
         for i in range(wide):
             q_copy(rel, i).wait()
@@ -274,7 +275,6 @@
 
     each(0, far, kv_arrived)
 
-    start_pair(3)
     visible = key_place <= q_place
     all_keys = kv_buf[0].reshape(key_count, HEAD_DIM)
     all_values = kv_buf[1].reshape(key_count, HEAD_DIM)
@@ -408,8 +408,8 @@
             p_from(n, source).wait_recv()
             head_sum = head_sum + p_recv2[n, source].astype(jnp.float32)
         att = (res_buf[:, cols].astype(jnp.float32) + head_sum).astype(jnp.bfloat16)
+        attended[:, cols] = att
         att = att.astype(jnp.float32)
-        attended[:, cols] = att
         gain = gain_buf[cols].astype(jnp.float32).reshape(1, width)
         x[n, 0, a] = (att * gain).astype(jnp.bfloat16)
         each(1, far, lambda i: x_far(n, i).start())
@@ -426,17 +426,17 @@
             p_on(step - 3)
         if 0 <= step - 7 < pieces:
             square = p_end(step - 7, square)
-        if step == pieces:
-            start_pair(4)
         if step >= pieces + 7 - AHEAD:
             x_pass(step - (pieces + 7 - AHEAD))
     inverse = lax.rsqrt(square / (pieces * width) + 1e-6)
     inv_buf[0, a] = jnp.broadcast_to(inverse, inv_buf.shape[2:])
     each(1, far, lambda i: inv_far(i).start())
     inv_beside(a).start()
-    start_pair(5)
 
     rows = 2 * far * quarter
+    units = hidden.shape[1]
+    size = TILE if units % TILE == 0 else units
+    tiles = [slice(first, first + size) for first in range(0, units, size)]
 
     def expand(k):
         @pl.when(k + AHEAD < pieces)
@@ -447,27 +447,25 @@
         def _():
             each(1, far, inv_pass)
 
-        @pl.when(k + 6 < pieces)
-        def _():
-            start_pair(k + 6)
-
-        @pl.when((k >= 1) & (k <= slots))
-        def _():
-            wd_copy(k - 1).start()
-
         wg_copy(k).wait()
         wu_copy(k).wait()
         each(0, far, lambda source: x_beside(k, source).wait_recv())
         piece = x[k].reshape(rows, width)
-        gate_acc[...] += jnp.dot(piece, wg[k], preferred_element_type=jnp.float32)
-        up_acc[...] += jnp.dot(piece, wu[k], preferred_element_type=jnp.float32)
+        for tile in tiles:
+            gate_acc[:, tile] += jnp.dot(
+                piece, wg[k, :, tile], preferred_element_type=jnp.float32
+            )
+            up_acc[:, tile] += jnp.dot(
+                piece, wu[k, :, tile], preferred_element_type=jnp.float32
+            )
 
     loop(pieces, expand)
     each(0, far, lambda source: inv_beside(source).wait_recv())
     scale = inv_buf[...].reshape(rows, inv_buf.shape[-1])[:, 0:1]
-    gate = gate_acc[...] * scale
-    up = up_acc[...] * scale
-    hidden[...] = (gate / (1.0 + jnp.exp(-gate)) * up).astype(jnp.bfloat16)
+    for tile in tiles:
+        gate = gate_acc[:, tile] * scale
+        up = up_acc[:, tile] * scale
+        hidden[:, tile] = (gate / (1.0 + jnp.exp(-gate)) * up).astype(jnp.bfloat16)
 
     def d_beside(n):
         return remote(d_send.at[n], d_recv.at[n], d_s1.at[n], d_r1.at[n], beside)
@@ -519,7 +517,7 @@
     for n in range(pieces):
         cols = slice(n * width, (n + 1) * width)
         gain = gain_buf[cols].astype(jnp.float32).reshape(1, width)
-        normed = (attended[:, cols] * inverse * gain).astype(jnp.bfloat16)
+        normed = (attended[:, cols].astype(jnp.float32) * inverse * gain).astype(jnp.bfloat16)
         logit_w = logit_buf[cols].astype(jnp.float32).reshape(1, width)
         logit = logit + jnp.sum(
             normed.astype(jnp.float32) * logit_w, axis=-1, keepdims=True
@@ -541,7 +539,7 @@
                 shared = add(i, shared)
         else:
             shared = lax.fori_loop(1, far, add, shared)
-        out[:, cols] = attended[:, cols] + gate_prob * shared
+        out[:, cols] = attended[:, cols].astype(jnp.float32) + gate_prob * shared
 
     for w in range(2):
         each(1, far, lambda i, w=w: kv_far(w, i).wait_send())
@@ -615,7 +613,7 @@
             pltpu.VMEM((proj_pieces, wide, quarter, PROJ), bf16),
             pltpu.VMEM((proj_pieces, wide, quarter, PROJ), bf16),
             pltpu.VMEM((proj_pieces, wide, quarter, PROJ), f32),
-            pltpu.VMEM((quarter, depth), f32),
+            pltpu.VMEM((quarter, depth), bf16),
             pltpu.VMEM((pieces, far, quarter, WIDTH), bf16),
             pltpu.VMEM((pieces, far, quarter, WIDTH), bf16),
             pltpu.VMEM((pieces, far, quarter, WIDTH), bf16),

time: 59.4 us -> 59.5 us (level)
  no operation moved by 1% of the time
where the time goes in v5:
time: 59.5 us; the launch traced here: 59.3 us
  Pallas kernels  57.7 us (97%)
  other arithmetic  1.6 us (3%)
    pallas_call x1, Pallas kernels, per_device(): pl.pallas_call(functools.partial(kernel, ctx_count, tp_count), out_shape=...  57.7 us
    convert_element_type x1, other arithmetic, per_device(): return layer_out.astype(bf16)  1.6 us

profile of v5, /device:TPU:0, one launch (start us, length us, event | category | flops | bytes accessed | tf_op | source)
XLA Modules:
  0.0 59.3 jit_solution(11151216958309363852)
XLA Ops:
  0.0 57.7 %layer.1 = f32[16,3584]{1,0:T(8,128)} custom-call(bf16[64,896]{1,0:T(8,128)(2,1)} %queries.1, bf16[64,128]{1,0:T(8,128)(2,1)} %keys.1, bf16[64,128]{1,0:T(8,128)(2,1)} %values.1, s32[8]{0:T(128)} %block_table.1, bf16[16,3584]{1,0:T(8,128)(2,1)} %residual.1, bf16[896,3584]{1,0:T(8,128)(2,1)} %out_weight.1, bf16[3584]{0:T(1024)(128)(2,1)} %norm_gain.1, ...), custom_call_target="tpu_custom_call" | custom-call | flops 7457472512 | bytes 61472768 | tf_op jit(solution)/shard_map/layer/pallas_call | solution.py:589
  57.7 1.6 %convert_element_type.3 = bf16[16,3584]{1,0:T(8,128)(2,1)} convert(f32[16,3584]{1,0:T(8,128)} %layer.1) | non-fusion elementwise | flops 57344 | bytes 344064 | tf_op jit(solution)/shard_map/convert_element_type | solution.py:674
